TPU v7x, 32 devices: a whole 2x2x4 slice. The times are simulated.
32 devices in a mesh: energy: 8 (over z, y), space: 4 (over x, core).
Axes of the slice: x: 2, y: 2, z: 4, core: 2. Of those that a mesh axis runs over, the one named last changes fastest.
Arguments:
- iso_green: bfloat16 [8, 8, 2, 192, 192], P('energy', 'space'), as said below
- coupling: bfloat16 [8, 192, 192], P('space')
- screened: bfloat16 [8, 8, 2, 192, 192], P('energy', 'space'), as said below
Outputs:
- sigma: bfloat16 [8, 8, 2, 192, 192], P('energy', 'space')
Inputs may be any that keep to these rules, and one draw needn't show every extreme that they name: `iso_green`: every complex [192, 192] block (real and imaginary parts) equals its own transpose. `screened`: every complex [192, 192] block (real and imaginary parts) equals its own transpose.
All inputs are finite; a program needn't handle non-finite values.
Results may differ from a plain program's by a relative error of at most 0.023.
Values may be sent and summed in bfloat16 or wider, within the bound.
A program may use at most 64 MiB of HBM per device.

v0:
```python
import math

import jax
import jax.numpy as jnp
from jax import lax
from jax.sharding import PartitionSpec as P


def prefix_2(shard, axis, join, neutral):
    place = lax.axis_index(axis)
    gathered = jax.tree.map(
        lambda a, kind: lax.all_gather(a.astype(kind), axis),
        shard,
        jax.tree.map(lambda a: jnp.bfloat16 if a.dtype == jnp.float32 else a.dtype, shard),
    )
    state = jax.tree.map(lambda a, e: jnp.zeros_like(a) + jnp.asarray(e, a.dtype), shard, neutral)

    def one(turn, state):
        return join(
            state,
            jax.tree.map(
                lambda a, own: lax.dynamic_index_in_dim(a, turn, 0, False).astype(own.dtype),
                gathered,
                shard,
            ),
        )

    return lax.fori_loop(0, place, one, state)


def complex_product(operand, factor, pattern):
    left = jnp.concatenate([operand[:, 0], operand[:, 1]], axis=-1)
    fa_re = factor[:, 0]
    fa_im = factor[:, 1]
    if pattern == "ekl,eml->ekm":
        right_re = jnp.concatenate([fa_re, -fa_im], axis=-1)
        right_im = jnp.concatenate([fa_im, fa_re], axis=-1)
        right = jnp.stack([right_re, right_im], axis=1)
        return jnp.einsum("ekl,ecml->eckm", left, right, preferred_element_type=jnp.float32)
    right_re = jnp.concatenate([fa_re, -fa_im], axis=-2)
    right_im = jnp.concatenate([fa_im, fa_re], axis=-2)
    right = jnp.stack([right_re, right_im], axis=1)
    return jnp.einsum("ekl,eclm->eckm", left, right, preferred_element_type=jnp.float32)


def sandwich(carried, factor, source):
    middle = complex_product(carried, factor, "ekl,eml->ekm").astype(jnp.bfloat16)
    return (source.astype(jnp.float32) + complex_product(factor, middle, "ekl,elm->ekm")).astype(
        jnp.bfloat16
    )


def compose(earlier, latter):
    joined = complex_product(latter[0], earlier[0], "ekl,elm->ekm").astype(jnp.bfloat16)
    return (joined, sandwich(earlier[1], latter[0], latter[1]))


def fold_step(carried, inputs):
    return (compose(carried, inputs), None)


def apply_step(carried, inputs):
    updated = sandwich(carried, inputs[0], inputs[1])
    return (updated, updated)


def twiddle_tables(points):
    index_row = lax.iota(jnp.int32, points)
    phase_index = index_row[:, None] * index_row[None, :] % points
    angles = phase_index.astype(jnp.float32) * (2.0 * math.pi / points)
    return jnp.concatenate([jnp.cos(angles), jnp.sin(angles)], axis=0)


def convolve(operands):
    green_part, screen_part = operands
    points = green_part.shape[0]
    kept_shape = green_part.shape
    table = twiddle_tables(points)
    table_high = table.astype(jnp.bfloat16)
    table_rest = (table - table_high.astype(jnp.float32)).astype(jnp.bfloat16)
    green_flat = green_part.reshape(points, 2, -1)
    screen_flat = screen_part.reshape(points, 2, -1)
    width = green_flat.shape[2]
    joined = jnp.concatenate(
        [green_flat[:, 0], green_flat[:, 1], screen_flat[:, 0], screen_flat[:, 1]], axis=1
    )
    mixed = jnp.dot(table_high, joined, preferred_element_type=jnp.float32) + jnp.dot(
        table_rest, joined, preferred_element_type=jnp.float32
    )
    with_cos = mixed[:points]
    with_sin = mixed[points:]
    green_re = with_cos[:, :width] + with_sin[:, width : 2 * width]
    green_im = with_cos[:, width : 2 * width] - with_sin[:, :width]
    screen_re = with_cos[:, 2 * width : 3 * width] + with_sin[:, 3 * width :]
    screen_im = with_cos[:, 3 * width :] - with_sin[:, 2 * width : 3 * width]
    prod_re = green_re * screen_re - green_im * screen_im
    prod_im = green_re * screen_im + green_im * screen_re
    spectrum = jnp.concatenate([prod_re, prod_im], axis=1)
    back = jnp.dot(table, spectrum, precision=lax.Precision.HIGH)
    back_cos = back[:points]
    back_sin = back[points:]
    back_re = back_cos[:, :width] - back_sin[:, width:]
    back_im = back_cos[:, width:] + back_sin[:, :width]
    scaling = 1.0 / (points * math.sqrt(points))
    result = (
        jnp.concatenate([-back_im * scaling, back_re * scaling], axis=1)
        .reshape(kept_shape)
        .astype(jnp.bfloat16)
    )
    return lax.all_to_all(result, "energy", split_axis=0, concat_axis=2, tiled=True)


def shards(iso_green, coupling, screened):
    energies = iso_green.shape[0]
    blocks = iso_green.shape[1]
    order = iso_green.shape[3]
    groups = lax.axis_size("energy")
    green_blocks = jnp.moveaxis(iso_green, 1, 0)
    transfer_blocks = jnp.einsum(
        "ebckl,blm->beckm", iso_green, coupling, preferred_element_type=jnp.float32
    ).astype(jnp.bfloat16)
    initial_map = (transfer_blocks[0], green_blocks[0])
    aggregate = lax.scan(fold_step, initial_map, (transfer_blocks[1:], green_blocks[1:]))[0]
    unit_matrix = jnp.broadcast_to(jnp.eye(order, dtype=jnp.bfloat16), (energies, order, order))
    identity_map = (
        jnp.stack([unit_matrix, jnp.zeros_like(unit_matrix)], axis=1),
        jnp.zeros_like(aggregate[1]),
    )
    prefix = prefix_2(aggregate, "space", compose, identity_map)
    connected = lax.scan(apply_step, prefix[1], (transfer_blocks, green_blocks))[1]
    stacked_green = connected.transpose(1, 2, 0, 3, 4).reshape(energies, 2, blocks, order * order)
    stacked_screen = screened.transpose(0, 2, 1, 3, 4).reshape(energies, 2, blocks, order * order)
    green_sent = stacked_green.reshape(energies, 2, groups, -1)
    screen_sent = stacked_screen.reshape(energies, 2, groups, -1)
    returned = convolve(
        (
            lax.all_to_all(green_sent, "energy", split_axis=2, concat_axis=0, tiled=True),
            lax.all_to_all(screen_sent, "energy", split_axis=2, concat_axis=0, tiled=True),
        )
    )
    returned = returned.reshape(energies, 2, blocks, -1)
    return returned.reshape(energies, 2, blocks, order, order).transpose(0, 2, 1, 3, 4)


def solution(mesh):
    in_specs = (
        P("energy", "space", None, None, None),
        P("space", None, None),
        P("energy", "space", None, None, None),
    )
    out_specs = P("energy", "space", None, None, None)
    return jax.shard_map(shards, mesh=mesh, in_specs=in_specs, out_specs=out_specs, check_vma=False)
```

profile of v0, /device:TPU:2, one launch (start us, length us, event | category | flops | bytes accessed | tf_op | source)
XLA Modules:
  0.0 79.1 jit_solution(9900939300222932028)
XLA Ops:
  0.0 0.9 %copy-done = bf16[2,192,192]{2,1,0:T(8,128)(2,1)S(1)} copy-done((bf16[2,192,192]{2,1,0:T(8,128)(2,1)S(1)}, bf16[2,192,192]{2,1,0:T(8,128)(2,1)}, u32[]{:S(2)}) %copy-start) | copy-done | bytes 147480
  0.9 1.2 %convolution_convert_fusion.2 = bf16[2,2,192,192]{3,2,1,0:T(8,128)(2,1)S(1)} fusion(bf16[1,2,2,192,192]{4,3,2,1,0:T(8,128)(2,1)} %param.7, bf16[2,192,192]{2,1,0:T(8,128)(2,1)S(1)} %copy-done), kind=kOutput, calls=%fused_computation.69 | convolution fusion | flops 56770560 | bytes 737280 | tf_op jit(solution)/shard_map/ebckl,blm->beckm/dot_general | solution.py:119
  2.4 0.4 fusion.36
  2.8 0.2 copy.52
  3.2 0.4 fusion.35
  3.5 0.1 copy.53
  3.7 8.2 %all-gather = bf16[4,2,192,192]{3,2,1,0:T(8,128)(2,1)S(1)} all-gather(bf16[1,2,192,192]{3,2,1,0:T(8,128)(2,1)S(1)} %copy.53), channel_id=2, replica_groups=mesh['energy'=8,'space'=4] {'space'}, dimensions={0}, use_global_device_ids=true | all-gather | bytes 737280 | tf_op jit(solution)/shard_map/all_gather | solution.py:12
  11.9 0.4 fusion.37
  12.3 0.1 copy.55
  12.4 8.7 %all-gather.1 = bf16[4,2,192,192]{3,2,1,0:T(8,128)(2,1)S(1)} all-gather(bf16[1,2,192,192]{3,2,1,0:T(8,128)(2,1)S(1)} %copy.55), channel_id=3, replica_groups=mesh['energy'=8,'space'=4] {'space'}, dimensions={0}, use_global_device_ids=true | all-gather | bytes 737280 | tf_op jit(solution)/shard_map/all_gather | solution.py:12
  21.2 2.9 %while.8 = (s32[]{:T(128)}, bf16[1,2,192,192]{2,3,1,0:T(8,128)(2,1)S(1)}, s32[]{:T(128)}, bf16[4,1,2,192,192]{4,3,2,0,1:T(8,128)(2,1)S(1)}, bf16[4,1,2,192,192]{...) while((s32[]{:T(128)}, bf16[1,2,192,192]{2,3,1,0:T(8,128)(2,1)S(1)}, s32[]{:T(128)}, ...), condition=%wide.region_1.2_spmd, body=%wide.region_0.1_spmd.sunk | while | flops 115679232 | bytes 4718719 | solution.py:28
  21.3 0.1 fusion.95
  21.4 0.1 copy.79
  21.6 0.4 fusion.96
  22.1 0.1 copy.80
  22.3 0.4 fusion.98
  22.7 0.1 fusion.95
  22.9 0.1 copy.79
  23.0 0.4 fusion.96
  23.6 0.1 copy.80
  23.7 0.4 fusion.98
  24.1 4.9 %while.30 = (s32[]{:T(128)}, bf16[1,2,192,192]{2,3,1,0:T(8,128)(2,1)S(1)}, bf16[2,1,2,192,192]{3,4,2,1,0:T(8,128)(2,1)}, bf16[2,1,2,192,192]{3,4,2,1,0:T(8,128)(...) while((s32[]{:T(128)}, bf16[1,2,192,192]{2,3,1,0:T(8,128)(2,1)S(1)}, ...), condition=%wide.region_3.4_spmd, body=%wide.region_2.3_spmd.sunk | while | flops 115679232 | bytes 6832261 | solution.py:130
  24.3 0.1 copy.81
  24.5 0.4 fusion.101
  25.1 0.4 copy-done.3
  25.5 0.4 bitcast_dynamic-update-slice_fusion.2
  25.9 0.7 copy-done.4
  26.8 0.1 copy.81
  27.0 0.4 fusion.101
  27.5 0.4 copy-done.3
  27.9 0.4 bitcast_dynamic-update-slice_fusion.2
  28.3 0.7 copy-done.4
  29.0 1.2 %copy.60 = bf16[1,2,2,192,192]{4,3,2,1,0:T(8,128)(2,1)S(1)} copy(bf16[1,2,2,192,192]{3,4,1,0,2:T(8,128)(2,1)} %bitcast.312) | data formatting | bytes 589824 | tf_op jit(solution)/shard_map/transpose | solution.py:131
  30.3 0.4 reshape_reshape.9
  30.7 1.0 %copy.61 = bf16[1,2,8,9216]{3,1,0,2:T(2,128)(2,1)} copy(bf16[1,2,8,9216]{3,2,1,0:T(8,128)(2,1)S(1)} %reshape_reshape.9) | data formatting | bytes 589824 | tf_op jit(solution)/shard_map/reshape;reshape | solution.py:133
  31.7 5.8 %all-to-all-start = ((bf16[1,2,8,9216]{3,1,0,2:T(2,128)(2,1)}), bf16[1,2,8,9216]{3,1,0,2:T(2,128)(2,1)S(1)}, u32[]{:S(2)}, u32[]{:S(2)}) async-start(bf16[1,2,8,9216]{3,1,0,2:T(2,128)(2,1)} %copy.61), calls=%async_computation | async-start | bytes 589824 | tf_op jit(solution)/shard_map/all_to_all | solution.py:137
  37.6 0.4 reshape_reshape.10
  37.9 1.0 %copy.64 = bf16[1,2,8,9216]{3,1,0,2:T(2,128)(2,1)} copy(bf16[1,2,8,9216]{3,2,1,0:T(8,128)(2,1)S(1)} %reshape_reshape.10) | data formatting | bytes 589824 | tf_op jit(solution)/shard_map/reshape;reshape | solution.py:134
  39.0 9.0 %all-to-all-done = bf16[1,2,8,9216]{3,1,0,2:T(2,128)(2,1)S(1)} async-done(((bf16[1,2,8,9216]{3,1,0,2:T(2,128)(2,1)}), bf16[1,2,8,9216]{3,1,0,2:T(2,128)(2,1)S(1)}, u32[]{:S(2)}, u32[]{:S(2)}) %all-to-all-start) | async-done | bytes 294944 | tf_op jit(solution)/shard_map/all_to_all | solution.py:137
  48.0 4.1 %all-to-all-start.1 = ((bf16[1,2,8,9216]{3,1,0,2:T(2,128)(2,1)}), bf16[1,2,8,9216]{3,1,0,2:T(2,128)(2,1)S(1)}, u32[]{:S(2)}, u32[]{:S(2)}) async-start(bf16[1,2,8,9216]{3,1,0,2:T(2,128)(2,1)} %copy.64), calls=%async_computation.1 | async-start | bytes 589824 | tf_op jit(solution)/shard_map/all_to_all | solution.py:138
  52.2 9.8 %all-to-all-done.1 = bf16[1,2,8,9216]{3,1,0,2:T(2,128)(2,1)S(1)} async-done(((bf16[1,2,8,9216]{3,1,0,2:T(2,128)(2,1)}), bf16[1,2,8,9216]{3,1,0,2:T(2,128)(2,1)S(1)}, u32[]{:S(2)}, u32[]{:S(2)}) %all-to-all-start.1) | async-done | bytes 294944 | tf_op jit(solution)/shard_map/all_to_all | solution.py:138
  62.0 0.4 fusion.59
  62.5 0.4 convolution_add_fusion
  63.0 0.6 fusion.38
  63.8 0.3 copy.66
  64.1 13.7 %all_to_all.45 = bf16[8,2,1,9216]{3,1,2,0:T(2,128)(2,1)S(1)} all-to-all(bf16[8,2,1,9216]{3,1,2,0:T(2,128)(2,1)S(1)} %copy.66), channel_id=1, replica_groups=mesh['energy'=8,'space'=4] {'energy'}, dimensions={0} | all-to-all | bytes 589824 | tf_op jit(solution)/shard_map/all_to_all | solution.py:110
  77.8 0.5 reshape_reshape.11
  78.3 0.8 copy.68
  (62 shorter events, 2.1 us)
Async XLA Ops:
  0.0 0.9 %copy-start = (bf16[2,192,192]{2,1,0:T(8,128)(2,1)S(1)}, bf16[2,192,192]{2,1,0:T(8,128)(2,1)}, u32[]{:S(2)}) copy-start(bf16[2,192,192]{2,1,0:T(8,128)(2,1)} %param.8) | copy-start | bytes 442372
  0.0 2.2 %copy-start.1 = (bf16[1,2,2,192,192]{4,3,2,1,0:T(8,128)(2,1)S(1)}, bf16[1,2,2,192,192]{4,3,2,1,0:T(8,128)(2,1)}, u32[]{:S(2)}) copy-start(bf16[1,2,2,192,192]{4,3,2,1,0:T(8,128)(2,1)} %param.7) | copy-start | bytes 884740
  24.5 1.0 %copy-start.3 = (bf16[2,1,2,192,192]{3,4,2,1,0:T(8,128)(2,1)S(1)}, bf16[2,1,2,192,192]{3,4,2,1,0:T(8,128)(2,1)}, u32[]{:S(2)}) copy-start(bf16[2,1,2,192,192]{3,4,2,1,0:T(8,128)(2,1)} %get-tuple-element.340) | copy-start | bytes 884740 | tf_op jit(solution)/shard_map/while
  25.8 0.7 copy-start.4
  26.9 1.0 %copy-start.3 = (bf16[2,1,2,192,192]{3,4,2,1,0:T(8,128)(2,1)S(1)}, bf16[2,1,2,192,192]{3,4,2,1,0:T(8,128)(2,1)}, u32[]{:S(2)}) copy-start(bf16[2,1,2,192,192]{3,4,2,1,0:T(8,128)(2,1)} %get-tuple-element.340) | copy-start | bytes 884740 | tf_op jit(solution)/shard_map/while
  28.3 0.7 copy-start.4
  29.0 8.5 %copy-start.2 = (bf16[1,2,2,192,192]{4,3,2,1,0:T(8,128)(2,1)S(1)}, bf16[1,2,2,192,192]{4,3,2,1,0:T(8,128)(2,1)}, u32[]{:S(2)}) copy-start(bf16[1,2,2,192,192]{4,3,2,1,0:T(8,128)(2,1)} %param.9) | copy-start | bytes 884740
  31.7 16.3 %all-to-all-start = ((bf16[1,2,8,9216]{3,1,0,2:T(2,128)(2,1)}), bf16[1,2,8,9216]{3,1,0,2:T(2,128)(2,1)S(1)}, u32[]{:S(2)}, u32[]{:S(2)}) async-start(bf16[1,2,8,9216]{3,1,0,2:T(2,128)(2,1)} %copy.61), calls=%async_computation | async-start | bytes 589824 | tf_op jit(solution)/shard_map/all_to_all | solution.py:137
  48.0 13.9 %all-to-all-start.1 = ((bf16[1,2,8,9216]{3,1,0,2:T(2,128)(2,1)}), bf16[1,2,8,9216]{3,1,0,2:T(2,128)(2,1)S(1)}, u32[]{:S(2)}, u32[]{:S(2)}) async-start(bf16[1,2,8,9216]{3,1,0,2:T(2,128)(2,1)} %copy.64), calls=%async_computation.1 | async-start | bytes 589824 | tf_op jit(solution)/shard_map/all_to_all | solution.py:138
where the time goes:
time: 79.6 us; the launch traced here: 79.1 us
  blocking collectives  30.6 us (38%)
  waiting for transfers between devices  18.8 us (24%)
  local copies, waits for them, and re-layouts  10.7 us (13%)
  starting transfers between devices  9.92 us (12%)
  matrix products  6.66 us (8%)
  other arithmetic  1.69 us (2%)
    all_gather x2, blocking collectives, prefix_2(): lax.all_gather(a.astype(kind), axis)  16.9 us
    all_to_all x1, blocking collectives, convolve(): lax.all_to_all(result, 'energy', split_axis=0, concat_axis=2, tiled=True)  13.7 us
    all_to_all x1, waiting for transfers between devices, shards(): lax.all_to_all(screen_sent, 'energy', split_axis=2, concat_axis=0, tiled=...  9.77 us
    all_to_all x1, waiting for transfers between devices, shards(): lax.all_to_all(green_sent, 'energy', split_axis=2, concat_axis=0, tiled=T...  8.99 us
    all_to_all x1, starting transfers between devices, shards(): lax.all_to_all(green_sent, 'energy', split_axis=2, concat_axis=0, tiled=T...  5.84 us
    all_to_all x1, starting transfers between devices, shards(): lax.all_to_all(screen_sent, 'energy', split_axis=2, concat_axis=0, tiled=...  4.09 us
    while x8, local copies, waits for them, and re-layouts  2.34 us
    dot_general x6, matrix products, complex_product(): jnp.einsum('ekl,eclm->eckm', left, right, preferred_element_type=jnp.floa...  2.14 us
  transfers between devices with their start and end apart: 2, of which 2 were waited for; matrix products, arithmetic and copies ran while one was open for 2% of the time, Pallas kernels for 0%

commit v1 on v0

v1 whole, which is shorter than its diff:
```python
import functools
import math

import jax
import jax.numpy as jnp
from jax import lax
from jax.experimental import pallas as pl
from jax.experimental.pallas import tpu as pltpu
from jax.sharding import PartitionSpec as P

MESH = pl.DeviceIdType.MESH
BF16 = jnp.bfloat16
F32 = jnp.float32
UNROLL = 8


def loop(low, high, body):
    if high - low <= UNROLL:
        for step in range(low, high):
            body(step)
    else:

        def one(step, carry):
            body(step)
            return carry

        lax.fori_loop(low, high, one, 0)


def dot(a, b):
    return jnp.dot(a, b, preferred_element_type=F32)


def dot_tn(a, b):
    return lax.dot_general(a, b, (((0,), (0,)), ((), ())), preferred_element_type=F32)


def product(a, b, mul=dot):
    real = mul(a[0], b[0]) - mul(a[1], b[1])
    imag = mul(a[0], b[1]) + mul(a[1], b[0])
    return real, imag


def rounded(pair):
    return pair[0].astype(BF16), pair[1].astype(BF16)


def load(ref, *at):
    return ref[(*at, 0)], ref[(*at, 1)]


def store(ref, pair, *at):
    ref[(*at, 0)] = pair[0].astype(BF16)
    ref[(*at, 1)] = pair[1].astype(BF16)


def sandwich(source, left, inner, right):
    outer = product(left, rounded(product(inner, right)))
    return source[0].astype(F32) + outer[0], source[1].astype(F32) + outer[1]


def pack(ref, plane, start, whole):
    t = whole.shape[0] // 3
    ref[plane, start : start + t] = whole[2 * t :, : 2 * t].astype(BF16)
    ref[plane, start + t : start + 2 * t] = whole[:t, : 2 * t].astype(BF16)
    corner = jnp.concatenate([whole[2 * t :, 2 * t :], whole[t : 2 * t, t : 2 * t]], axis=1)
    ref[plane, start + 2 * t : start + 3 * t] = corner.astype(BF16)


def unpack(ref, at, rows):
    t = rows.shape[0] // 3
    low, top, corner = rows[:t], rows[t : 2 * t], rows[2 * t :]
    flipped = top.astype(F32).T[t:].astype(BF16)
    ref[(*at, slice(2 * t, 3 * t), slice(0, 2 * t))] = low
    ref[(*at, slice(2 * t, 3 * t), slice(2 * t, 3 * t))] = corner[:, :t]
    ref[(*at, slice(0, t), slice(0, 2 * t))] = top
    ref[(*at, slice(t, 2 * t), slice(0, 2 * t))] = jnp.concatenate(
        [flipped, corner[:, t:]], axis=1
    )
    ref[(*at, slice(0, 2 * t), slice(2 * t, 3 * t))] = low.astype(F32).T.astype(BF16)


def kernel(
    groups,
    places,
    iso_ref,
    coupling_ref,
    screened_ref,
    out_ref,
    green,
    hop,
    screen,
    maps,
    maps_t,
    conn,
    pair_conn,
    pair_map,
    carry_packed,
    carry,
    green_send,
    screen_send,
    green_recv,
    screen_recv,
    green_wide,
    screen_wide,
    sigma_send,
    sigma_recv,
    load_sem,
    pair_sem,
    carry_sem,
    trade_sem,
    exchange_sem,
):
    blocks = green.shape[0]
    order = green.shape[-1]
    chunk = green_recv.shape[2]
    last = blocks - 1
    me = lax.axis_index("energy")
    place = lax.axis_index("space")
    pair = place // 2
    side = place % 2
    odd = side == 1
    partner = place + 1 - 2 * side
    pairs = places // 2

    loads = [
        pltpu.make_async_copy(iso_ref.at[0], green, load_sem.at[0]),
        pltpu.make_async_copy(coupling_ref, hop, load_sem.at[1]),
        pltpu.make_async_copy(screened_ref.at[0], screen, load_sem.at[2]),
    ]
    for copy in loads:
        copy.start()

    barrier = pltpu.get_barrier_semaphore()

    def greet(step):
        pl.semaphore_signal(
            barrier, inc=1, device_id={"energy": (me + step) % groups}, device_id_type=MESH
        )

    loop(1, groups, greet)
    pl.semaphore_signal(barrier, inc=1, device_id={"space": partner}, device_id_type=MESH)
    sends_on = jnp.logical_and(odd, pair < pairs - 1)

    @pl.when(sends_on)
    def _():
        for plane in range(2):
            pl.semaphore_signal(
                barrier, inc=1, device_id={"space": place + 1 + plane}, device_id_type=MESH
            )

    @pl.when(pair > 0)
    def _():
        pl.semaphore_signal(barrier, inc=1, device_id={"space": 2 * pair - 1}, device_id_type=MESH)

    def exchange(index, source, target, step):
        to = (me + step) % groups
        return pltpu.make_async_remote_copy(
            src_ref=source(to),
            dst_ref=target,
            send_sem=exchange_sem.at[2 * index],
            recv_sem=exchange_sem.at[2 * index + 1],
            device_id={"energy": to},
            device_id_type=MESH,
        )

    def spread(ref):
        return lambda to: ref.at[:, pl.ds(pl.multiple_of(to * chunk, 16), chunk), :]

    def whole(index):
        part = green_recv.at[pl.ds(0, groups - 1)]
        return pltpu.make_async_remote_copy(
            src_ref=part,
            dst_ref=part,
            send_sem=exchange_sem.at[2 * index],
            recv_sem=exchange_sem.at[2 * index + 1],
            device_id={"energy": (me + 1) % groups},
            device_id_type=MESH,
        )

    pair_copies = [
        pltpu.make_async_remote_copy(
            src_ref=source,
            dst_ref=target,
            send_sem=pair_sem.at[2 * index],
            recv_sem=pair_sem.at[2 * index + 1],
            device_id={"space": partner},
            device_id_type=MESH,
        )
        for index, (source, target) in enumerate(
            [(conn.at[last], pair_conn), (maps.at[last], pair_map)]
        )
    ]

    def onward(plane):
        return pltpu.make_async_remote_copy(
            src_ref=green_send.at[plane, last * order : blocks * order],
            dst_ref=carry_packed.at[plane],
            send_sem=carry_sem.at[plane],
            recv_sem=carry_sem.at[2],
            device_id={"space": place + 1 + plane},
            device_id_type=MESH,
        )

    trade = pltpu.make_async_remote_copy(
        src_ref=carry_packed.at[side],
        dst_ref=carry_packed.at[side],
        send_sem=trade_sem.at[0],
        recv_sem=trade_sem.at[1],
        device_id={"space": partner},
        device_id_type=MESH,
    )

    loads[0].wait()
    loads[1].wait()

    def steps_of(block):
        kept = load(green, block)
        hopping = hop[block]
        ahead = (dot(kept[0], hopping).astype(BF16), dot(kept[1], hopping).astype(BF16))
        behind = (dot_tn(hopping, kept[0]).astype(BF16), dot_tn(hopping, kept[1]).astype(BF16))
        return ahead, behind

    store(conn, load(green, 0), 0)
    for block in range(1, blocks):
        ahead, behind = steps_of(block)
        store(maps, ahead, block)
        store(maps_t, behind, block)
        store(
            conn, sandwich(load(green, block), ahead, load(conn, block - 1), behind), block
        )

    pl.semaphore_wait(
        barrier,
        groups
        + 2 * jnp.where(sends_on, 1, 0).astype(jnp.int32)
        + jnp.where(pair > 0, 1, 0).astype(jnp.int32),
    )

    @pl.when(side == 0)
    def _():
        pair_copies[0].start()

    @pl.when(jnp.logical_or(odd, pair > 0))
    def _():
        ahead, behind = steps_of(0)
        store(maps, ahead, 0)
        store(maps_t, behind, 0)
        for block in range(1, blocks):
            before, before_t = load(maps, block - 1), load(maps_t, block - 1)
            ahead, behind = load(maps, block), load(maps_t, block)
            store(maps, product(ahead, before), block)
            store(maps_t, product(before_t, behind), block)

    @pl.when(jnp.logical_and(side == 0, pair > 0))
    def _():
        pair_copies[1].start()

    loads[2].wait()
    for block in range(blocks):
        for plane in range(2):
            pack(screen_send, plane, block * order, screen[block, plane])
    used = blocks * order
    if groups * chunk > used:
        for ref in (screen_send, green_send):
            ref[:, used:] = jnp.zeros((2, groups * chunk - used, ref.shape[2]), BF16)
    loop(
        1, groups, lambda step: exchange(0, spread(screen_send), screen_recv.at[me], step).start()
    )

    @pl.when(odd)
    def _():
        pair_copies[0].wait_recv()
        below = load(pair_conn)
        for block in reversed(range(blocks)):
            ahead, behind = load(maps, block), load(maps_t, block)
            store(conn, sandwich(load(conn, block), ahead, below, behind), block)

        @pl.when(pair > 0)
        def _():
            pair_copies[1].wait_recv()
            before = load(pair_map)
            for block in range(blocks):
                ahead, behind = load(maps, block), load(maps_t, block)
                store(maps, product(ahead, before), block)
                store(maps_t, product(before, behind, dot_tn), block)

    @pl.when(side == 0)
    def _():
        pair_copies[0].wait_send()

        @pl.when(pair > 0)
        def _():
            pair_copies[1].wait_send()

    @pl.when(pair > 0)
    def _():
        pltpu.make_async_remote_copy(
            src_ref=carry_packed.at[side],
            dst_ref=carry_packed.at[side],
            send_sem=carry_sem.at[0],
            recv_sem=carry_sem.at[2],
            device_id={"space": partner},
            device_id_type=MESH,
        ).wait_recv()
        trade.start()
        trade.wait()
        for plane in range(2):
            unpack(carry, (plane,), carry_packed[plane])

    for block in reversed(range(blocks)):

        @pl.when(pair > 0)
        def _():
            ahead, behind = load(maps, block), load(maps_t, block)
            store(conn, sandwich(load(conn, block), ahead, load(carry), behind), block)

        for plane in range(2):
            pack(green_send, plane, block * order, conn[block, plane])
        if block == last:

            @pl.when(sends_on)
            def _():
                for plane in range(2):
                    onward(plane).start()

    loop(1, groups, lambda step: exchange(1, spread(green_send), green_recv.at[me], step).start())
    mine = pl.ds(pl.multiple_of(me * chunk, 16), chunk)
    green_recv[me] = green_send[:, mine]
    screen_recv[me] = screen_send[:, mine]

    whole(0).wait_recv()

    def widen_screen(energy):
        screen_wide[energy] = screen_recv[energy].astype(F32)

    def widen_green(energy):
        green_wide[energy] = green_recv[energy].astype(F32)

    loop(0, groups, widen_screen)
    whole(1).wait_recv()
    loop(0, groups, widen_green)
    scale = 1.0 / math.sqrt(groups)

    def convolved(energy):
        def term(other, total):
            shift = (energy - other + groups) % groups
            g_re, g_im = green_wide[other, 0], green_wide[other, 1]
            s_re, s_im = screen_wide[shift, 0], screen_wide[shift, 1]
            return (
                total[0] + g_re * s_re - g_im * s_im,
                total[1] + g_re * s_im + g_im * s_re,
            )

        zero = jnp.zeros(green_wide.shape[2:], F32)
        total = (zero, zero)
        if groups <= UNROLL:
            for other in range(groups):
                total = term(other, total)
        else:
            total = lax.fori_loop(0, groups, term, total)
        return (total[1] * -scale).astype(BF16), (total[0] * scale).astype(BF16)

    def back(step):
        energy = (me + step) % groups
        real, imag = convolved(energy)
        sigma_send[step, 0] = real
        sigma_send[step, 1] = imag
        exchange(2, lambda to: sigma_send.at[step], spread(sigma_recv)(me), step).start()

    loop(1, groups, back)
    real, imag = convolved(me)
    sigma_recv[0, mine] = real
    sigma_recv[1, mine] = imag
    whole(2).wait_recv()
    for block in range(blocks):
        for plane in range(2):
            unpack(
                out_ref, (0, block, plane), sigma_recv[plane, block * order : (block + 1) * order]
            )

    for index in range(3):
        whole(index).wait_send()

    @pl.when(sends_on)
    def _():
        for plane in range(2):
            onward(plane).wait_send()


def shards(groups, places, iso_green, coupling, screened):
    blocks, order = iso_green.shape[1], iso_green.shape[3]
    tile = order // 3
    width = 2 * tile
    used = blocks * order
    chunk = 16 * -(-used // (16 * groups))
    full = (2, order, order)
    any_spec = pl.BlockSpec(memory_space=pl.ANY)
    return pl.pallas_call(
        functools.partial(kernel, groups, places),
        out_shape=jax.ShapeDtypeStruct(iso_green.shape, BF16),
        in_specs=[any_spec] * 3,
        out_specs=pl.BlockSpec(memory_space=pltpu.VMEM),
        scratch_shapes=[
            pltpu.VMEM((blocks, *full), BF16),
            pltpu.VMEM((blocks, order, order), BF16),
            pltpu.VMEM((blocks, *full), BF16),
            pltpu.VMEM((blocks, *full), BF16),
            pltpu.VMEM((blocks, *full), BF16),
            pltpu.VMEM((blocks, *full), BF16),
            pltpu.VMEM(full, BF16),
            pltpu.VMEM(full, BF16),
            pltpu.VMEM((2, order, width), BF16),
            pltpu.VMEM(full, BF16),
            pltpu.VMEM((2, groups * chunk, width), BF16),
            pltpu.VMEM((2, groups * chunk, width), BF16),
            pltpu.VMEM((groups, 2, chunk, width), BF16),
            pltpu.VMEM((groups, 2, chunk, width), BF16),
            pltpu.VMEM((groups, 2, chunk, width), F32),
            pltpu.VMEM((groups, 2, chunk, width), F32),
            pltpu.VMEM((groups, 2, chunk, width), BF16),
            pltpu.VMEM((2, groups * chunk, width), BF16),
            pltpu.SemaphoreType.DMA((3,)),
            pltpu.SemaphoreType.DMA((4,)),
            pltpu.SemaphoreType.DMA((3,)),
            pltpu.SemaphoreType.DMA((2,)),
            pltpu.SemaphoreType.DMA((6,)),
        ],
        compiler_params=pltpu.CompilerParams(
            collective_id=0, has_side_effects=True, vmem_limit_bytes=32 * 1024 * 1024
        ),
    )(iso_green, coupling, screened)


def solution(mesh):
    groups, places = mesh.shape["energy"], mesh.shape["space"]
    spec = P("energy", "space", None, None, None)
    return jax.shard_map(
        functools.partial(shards, groups, places),
        mesh=mesh,
        in_specs=(spec, P("space", None, None), spec),
        out_specs=spec,
        check_vma=False,
    )
```

time: 79.6 us -> 27.2 us (0.34)
  blocking collectives: 30.6 us -> 0 us
  Pallas kernels: 0 us -> 23.3 us
  waiting for transfers between devices: 18.8 us -> 0 us
  starting transfers between devices: 9.92 us -> 0 us
  local copies, waits for them, and re-layouts: 10.7 us -> 3.67 us
  matrix products: 6.66 us -> 0 us
  other arithmetic: 1.69 us -> 0 us
    pallas_call x0 -> x1, Pallas kernels: none -> 23.3 us  [shards(): pl.pallas_call(functools.partial(kernel, groups, places), out_shape=jax.S...]
    all_to_all x2 -> x0, waiting for transfers between devices: 18.8 us -> none  [the longest x1 9.77 us: shards(): lax.all_to_all(screen_sent, 'energy', split_axis=2, concat_axis=0, tiled=...]
    all_gather x2 -> x0, blocking collectives: 16.9 us -> none  [prefix_2(): lax.all_gather(a.astype(kind), axis)]
    all_to_all x1 -> x0, blocking collectives: 13.7 us -> none  [convolve(): lax.all_to_all(result, 'energy', split_axis=0, concat_axis=2, tiled=True)]
    all_to_all x2 -> x0, starting transfers between devices: 9.92 us -> none  [the longest x1 5.84 us: shards(): lax.all_to_all(green_sent, 'energy', split_axis=2, concat_axis=0, tiled=T...]
    dot_general x15 -> x0, matrix products: 6.66 us -> none  [the longest x6 2.14 us: complex_product(): jnp.einsum('ekl,eclm->eckm', left, right, preferred_element_type=jnp.floa...]
    another operation x9 -> x0, local copies, waits for them, and re-layouts: 3.76 us -> none  [the longest x2 1.39 us: shards(): screen_sent = stacked_screen.reshape(energies, 2, groups, -1)]
    unnamed x7, local copies, waits for them, and re-layouts: 1.14 us -> 3.67 us
  transfers between devices with their start and end apart: 2 -> 0, of which waited for: 2 -> 0; matrix products, arithmetic and copies ran while one was open for 2% -> 0% of each run, Pallas kernels for 0% -> 0%
where the time goes in v1:
time: 27.2 us; the launch traced here: 27 us
  Pallas kernels  23.3 us (86%)
  local copies, waits for them, and re-layouts  3.67 us (13%)
    pallas_call x1, Pallas kernels, shards(): pl.pallas_call(functools.partial(kernel, groups, places), out_shape=jax.S...  23.3 us
    unnamed x7, local copies, waits for them, and re-layouts  3.67 us

profile of v1, /device:TPU:2, one launch (start us, length us, event | category | flops | bytes accessed | tf_op | source)
XLA Modules:
  0.0 27.0 jit_solution(14500125487986907168)
XLA Ops:
  0.0 0.0 copy-start
  0.0 1.0 %copy-done = bf16[1,2,2,192,192]{4,3,2,1,0:T(8,128)(2,1)S(1)} copy-done((bf16[1,2,2,192,192]{4,3,2,1,0:T(8,128)(2,1)S(1)}, bf16[1,2,2,192,192]{4,3,2,1,0:T(8,128)(2,1)}, u32[]{:S(2)}) %copy-start) | copy-done | bytes 294936
  1.0 0.0 copy-start.1
  1.0 1.0 %copy-done.1 = bf16[1,2,2,192,192]{4,3,2,1,0:T(8,128)(2,1)S(1)} copy-done((bf16[1,2,2,192,192]{4,3,2,1,0:T(8,128)(2,1)S(1)}, bf16[1,2,2,192,192]{4,3,2,1,0:T(8,128)(2,1)}, u32[]{:S(2)}) %copy-start.1) | copy-done | bytes 294936
  2.0 0.0 copy-start.2
  2.0 0.9 %copy-done.2 = bf16[2,192,192]{2,1,0:T(8,128)(2,1)S(1)} copy-done((bf16[2,192,192]{2,1,0:T(8,128)(2,1)S(1)}, bf16[2,192,192]{2,1,0:T(8,128)(2,1)}, u32[]{:S(2)}) %copy-start.2) | copy-done | bytes 147480
  2.9 23.3 %shard_map.37 = bf16[1,2,2,192,192]{4,3,2,1,0:T(8,128)(2,1)S(1)} custom-call(bf16[1,2,2,192,192]{4,3,2,1,0:T(8,128)(2,1)S(1)} %copy-done, bf16[2,192,192]{2,1,0:T(8,128)(2,1)S(1)} %copy-done.2, bf16[1,2,2,192,192]{4,3,2,1,0:T(8,128)(2,1)S(1)} %copy-done.1), custom_call_target="tpu_custom_call" | custom-call | tf_op jit(solution)/shard_map/pallas_call | solution.py:399
  26.2 0.7 %copy.5 = bf16[1,2,2,192,192]{4,3,2,1,0:T(8,128)(2,1)} copy(bf16[1,2,2,192,192]{4,3,2,1,0:T(8,128)(2,1)S(1)} %shard_map.37) | data formatting | bytes 589824
Async XLA Ops:
  0.0 1.0 %copy-start = (bf16[1,2,2,192,192]{4,3,2,1,0:T(8,128)(2,1)S(1)}, bf16[1,2,2,192,192]{4,3,2,1,0:T(8,128)(2,1)}, u32[]{:S(2)}) copy-start(bf16[1,2,2,192,192]{4,3,2,1,0:T(8,128)(2,1)} %iso_ref.1) | copy-start | bytes 884740
  1.0 1.0 %copy-start.1 = (bf16[1,2,2,192,192]{4,3,2,1,0:T(8,128)(2,1)S(1)}, bf16[1,2,2,192,192]{4,3,2,1,0:T(8,128)(2,1)}, u32[]{:S(2)}) copy-start(bf16[1,2,2,192,192]{4,3,2,1,0:T(8,128)(2,1)} %screened_ref.1) | copy-start | bytes 884740
  2.0 0.9 %copy-start.2 = (bf16[2,192,192]{2,1,0:T(8,128)(2,1)S(1)}, bf16[2,192,192]{2,1,0:T(8,128)(2,1)}, u32[]{:S(2)}) copy-start(bf16[2,192,192]{2,1,0:T(8,128)(2,1)} %coupling_ref.1) | copy-start | bytes 442372

commit v2 on v1

--- a/solution.py
+++ b/solution.py
@@ -285,16 +285,13 @@
                 store(maps, product(ahead, before), block)
                 store(maps_t, product(before, behind, dot_tn), block)
 
-    @pl.when(side == 0)
-    def _():
-        pair_copies[0].wait_send()
-
-        @pl.when(pair > 0)
+    @pl.when(pair > 0)
+    def _():
+        @pl.when(side == 0)
         def _():
+            pair_copies[0].wait_send()
             pair_copies[1].wait_send()
 
-    @pl.when(pair > 0)
-    def _():
         pltpu.make_async_remote_copy(
             src_ref=carry_packed.at[side],
             dst_ref=carry_packed.at[side],
@@ -382,6 +379,10 @@
     for index in range(3):
         whole(index).wait_send()
 
+    @pl.when(jnp.logical_and(side == 0, pair == 0))
+    def _():
+        pair_copies[0].wait_send()
+
     @pl.when(sends_on)
     def _():
         for plane in range(2):
@@ -395,7 +396,7 @@
     used = blocks * order
     chunk = 16 * -(-used // (16 * groups))
     full = (2, order, order)
-    any_spec = pl.BlockSpec(memory_space=pl.ANY)
+    any_spec = pl.BlockSpec(memory_space=pltpu.HBM)
     return pl.pallas_call(
         functools.partial(kernel, groups, places),
         out_shape=jax.ShapeDtypeStruct(iso_green.shape, BF16),

time: 27.2 us -> 27.2 us (level)
  no operation moved by 1% of the time
where the time goes in v2:
time: 27.2 us; the launch traced here: 27 us
  Pallas kernels  23.3 us (86%)
  local copies, waits for them, and re-layouts  3.67 us (13%)
    pallas_call x1, Pallas kernels, shards(): pl.pallas_call(functools.partial(kernel, groups, places), out_shape=jax.S...  23.3 us
    unnamed x7, local copies, waits for them, and re-layouts  3.67 us

profile of v2, /device:TPU:2, one launch (start us, length us, event | category | flops | bytes accessed | tf_op | source)
XLA Modules:
  0.0 27.0 jit_solution(5398911110410358383)
XLA Ops:
  0.0 0.0 copy-start
  0.0 1.0 %copy-done = bf16[1,2,2,192,192]{4,3,2,1,0:T(8,128)(2,1)S(1)} copy-done((bf16[1,2,2,192,192]{4,3,2,1,0:T(8,128)(2,1)S(1)}, bf16[1,2,2,192,192]{4,3,2,1,0:T(8,128)(2,1)}, u32[]{:S(2)}) %copy-start) | copy-done | bytes 294936
  1.0 0.0 copy-start.1
  1.0 1.0 %copy-done.1 = bf16[1,2,2,192,192]{4,3,2,1,0:T(8,128)(2,1)S(1)} copy-done((bf16[1,2,2,192,192]{4,3,2,1,0:T(8,128)(2,1)S(1)}, bf16[1,2,2,192,192]{4,3,2,1,0:T(8,128)(2,1)}, u32[]{:S(2)}) %copy-start.1) | copy-done | bytes 294936
  2.0 0.0 copy-start.2
  2.0 0.9 %copy-done.2 = bf16[2,192,192]{2,1,0:T(8,128)(2,1)S(1)} copy-done((bf16[2,192,192]{2,1,0:T(8,128)(2,1)S(1)}, bf16[2,192,192]{2,1,0:T(8,128)(2,1)}, u32[]{:S(2)}) %copy-start.2) | copy-done | bytes 147480
  2.9 23.3 %shard_map.37 = bf16[1,2,2,192,192]{4,3,2,1,0:T(8,128)(2,1)S(1)} custom-call(bf16[1,2,2,192,192]{4,3,2,1,0:T(8,128)(2,1)S(1)} %copy-done, bf16[2,192,192]{2,1,0:T(8,128)(2,1)S(1)} %copy-done.2, bf16[1,2,2,192,192]{4,3,2,1,0:T(8,128)(2,1)S(1)} %copy-done.1), custom_call_target="tpu_custom_call" | custom-call | tf_op jit(solution)/shard_map/pallas_call | solution.py:400
  26.2 0.7 %copy.5 = bf16[1,2,2,192,192]{4,3,2,1,0:T(8,128)(2,1)} copy(bf16[1,2,2,192,192]{4,3,2,1,0:T(8,128)(2,1)S(1)} %shard_map.37) | data formatting | bytes 589824
Async XLA Ops:
  0.0 1.0 %copy-start = (bf16[1,2,2,192,192]{4,3,2,1,0:T(8,128)(2,1)S(1)}, bf16[1,2,2,192,192]{4,3,2,1,0:T(8,128)(2,1)}, u32[]{:S(2)}) copy-start(bf16[1,2,2,192,192]{4,3,2,1,0:T(8,128)(2,1)} %iso_ref.1) | copy-start | bytes 884740
  1.0 1.0 %copy-start.1 = (bf16[1,2,2,192,192]{4,3,2,1,0:T(8,128)(2,1)S(1)}, bf16[1,2,2,192,192]{4,3,2,1,0:T(8,128)(2,1)}, u32[]{:S(2)}) copy-start(bf16[1,2,2,192,192]{4,3,2,1,0:T(8,128)(2,1)} %screened_ref.1) | copy-start | bytes 884740
  2.0 0.9 %copy-start.2 = (bf16[2,192,192]{2,1,0:T(8,128)(2,1)S(1)}, bf16[2,192,192]{2,1,0:T(8,128)(2,1)}, u32[]{:S(2)}) copy-start(bf16[2,192,192]{2,1,0:T(8,128)(2,1)} %coupling_ref.1) | copy-start | bytes 442372

commit v3 on v2

--- a/solution.py
+++ b/solution.py
@@ -428,7 +428,7 @@
             pltpu.SemaphoreType.DMA((6,)),
         ],
         compiler_params=pltpu.CompilerParams(
-            collective_id=0, has_side_effects=True, vmem_limit_bytes=32 * 1024 * 1024
+            collective_id=0, has_side_effects=True
         ),
     )(iso_green, coupling, screened)
 

time: 27.2 us -> 25.4 us (0.934)
  local copies, waits for them, and re-layouts: 3.67 us -> 1.77 us
    unnamed x7 -> x1, local copies, waits for them, and re-layouts: 3.67 us -> 1.77 us
where the time goes in v3:
time: 25.4 us; the launch traced here: 25.2 us
  Pallas kernels  23.4 us (92%)
  local copies, waits for them, and re-layouts  1.77 us (7%)
    pallas_call x1, Pallas kernels, shards(): pl.pallas_call(functools.partial(kernel, groups, places), out_shape=jax.S...  23.4 us
    unnamed x1, local copies, waits for them, and re-layouts  1.77 us

profile of v3, /device:TPU:2, one launch (start us, length us, event | category | flops | bytes accessed | tf_op | source)
XLA Modules:
  0.0 25.2 jit_solution(12365389309286459181)
XLA Ops:
  0.0 23.4 %shard_map.37 = bf16[1,2,2,192,192]{4,3,2,1,0:T(8,128)(2,1)} custom-call(bf16[1,2,2,192,192]{4,3,2,1,0:T(8,128)(2,1)} %iso_ref.1, bf16[2,192,192]{2,1,0:T(8,128)(2,1)} %coupling_ref.1, bf16[1,2,2,192,192]{4,3,2,1,0:T(8,128)(2,1)} %screened_ref.1), custom_call_target="tpu_custom_call" | custom-call | tf_op jit(solution)/shard_map/pallas_call | solution.py:400
  23.4 1.8 %copy.5 = bf16[1,2,2,192,192]{4,3,2,1,0:T(8,128)(2,1)} copy(bf16[1,2,2,192,192]{4,3,2,1,0:T(8,128)(2,1)} %shard_map.37) | data formatting | bytes 589824

commit v4 on v3

--- a/solution.py
+++ b/solution.py
@@ -370,11 +370,7 @@
     sigma_recv[0, mine] = real
     sigma_recv[1, mine] = imag
     whole(2).wait_recv()
-    for block in range(blocks):
-        for plane in range(2):
-            unpack(
-                out_ref, (0, block, plane), sigma_recv[plane, block * order : (block + 1) * order]
-            )
+    out_ref[...] = sigma_recv[:, :used]
 
     for index in range(3):
         whole(index).wait_send()
@@ -387,6 +383,15 @@
     def _():
         for plane in range(2):
             onward(plane).wait_send()
+
+
+def unfold(packed_ref, out_ref):
+    blocks, order = out_ref.shape[1], out_ref.shape[-1]
+    for block in range(blocks):
+        for plane in range(2):
+            unpack(
+                out_ref, (0, block, plane), packed_ref[plane, block * order : (block + 1) * order]
+            )
 
 
 def shards(groups, places, iso_green, coupling, screened):
@@ -397,9 +402,9 @@
     chunk = 16 * -(-used // (16 * groups))
     full = (2, order, order)
     any_spec = pl.BlockSpec(memory_space=pltpu.HBM)
-    return pl.pallas_call(
+    packed = pl.pallas_call(
         functools.partial(kernel, groups, places),
-        out_shape=jax.ShapeDtypeStruct(iso_green.shape, BF16),
+        out_shape=jax.ShapeDtypeStruct((2, used, width), BF16),
         in_specs=[any_spec] * 3,
         out_specs=pl.BlockSpec(memory_space=pltpu.VMEM),
         scratch_shapes=[
@@ -431,6 +436,12 @@
             collective_id=0, has_side_effects=True
         ),
     )(iso_green, coupling, screened)
+    return pl.pallas_call(
+        unfold,
+        out_shape=jax.ShapeDtypeStruct(iso_green.shape, BF16),
+        in_specs=[pl.BlockSpec(memory_space=pltpu.VMEM)],
+        out_specs=pl.BlockSpec(memory_space=pltpu.VMEM),
+    )(packed)
 
 
 def solution(mesh):

time: 25.4 us -> 25.2 us (level)
  local copies, waits for them, and re-layouts: 1.77 us -> 0 us
  Pallas kernels: 23.4 us -> 25.1 us
    pallas_call x0 -> x1, Pallas kernels: none -> 1.82 us  [shards(): pl.pallas_call(unfold, out_shape=jax.ShapeDtypeStruct(iso_green.shape, BF...]
    unnamed x1 -> x0, local copies, waits for them, and re-layouts: 1.77 us -> none
where the time goes in v4:
time: 25.2 us; the launch traced here: 25.1 us
  Pallas kernels  25.1 us (100%)
    pallas_call x1, Pallas kernels, shards(): pl.pallas_call(functools.partial(kernel, groups, places), out_shape=jax.S...  23.2 us
    pallas_call x1, Pallas kernels, shards(): pl.pallas_call(unfold, out_shape=jax.ShapeDtypeStruct(iso_green.shape, BF...  1.82 us

profile of v4, /device:TPU:2, one launch (start us, length us, event | category | flops | bytes accessed | tf_op | source)
XLA Modules:
  0.0 25.1 jit_solution(5701562459945369712)
XLA Ops:
  0.0 23.2 %shard_map.37.packed_ref = bf16[2,384,128]{2,1,0:T(8,128)(2,1)} custom-call(bf16[1,2,2,192,192]{4,3,2,1,0:T(8,128)(2,1)} %iso_ref.1, bf16[2,192,192]{2,1,0:T(8,128)(2,1)} %coupling_ref.1, bf16[1,2,2,192,192]{4,3,2,1,0:T(8,128)(2,1)} %screened_ref.1), custom_call_target="tpu_custom_call" | custom-call | tf_op jit(solution)/shard_map/pallas_call | solution.py:405
  23.2 1.8 %shard_map.38 = bf16[1,2,2,192,192]{4,3,2,1,0:T(8,128)(2,1)} custom-call(bf16[2,384,128]{2,1,0:T(8,128)(2,1)} %shard_map.37.packed_ref), custom_call_target="tpu_custom_call" | custom-call | tf_op jit(solution)/shard_map/pallas_call | solution.py:439
